TPU v7x, 32 devices: a whole 2x2x4 slice. The times are simulated.
32 devices in a mesh: pairs: 8 (over z, y), tensor: 4 (over x, core).
Axes of the slice: x: 2, y: 2, z: 4, core: 2. Of those that a mesh axis runs over, the one named last changes fastest.
Arguments:
- queries: bfloat16 [2048, 4096], P('pairs', 'tensor'), may hold values from -100 to 100
- key_rows: bfloat16 [2048, 4096], P('pairs', 'tensor'), may hold values from -3.5 to 3.5
- value_rows: bfloat16 [2048, 4096], P('pairs', 'tensor'), may hold values from -12 to 12
- pair_ids: int32 [2048], P('pairs'), may hold values from 0 to 8, as said below
- out_weight: bfloat16 [4096, 4096], P('tensor', 'pairs'), may hold values from -0.09375 to 0.09375
- residual: bfloat16 [1536, 4096], P('pairs', 'tensor'), may hold values from -6 to 6
Outputs:
- hidden_out: bfloat16 [1536, 4096], P('pairs', 'tensor')
Inputs may be any that keep to these rules, and one draw needn't show every extreme that they name: `pair_ids`: within each block of 256 rows the entries never fall; rows with a value below 8 come first and rows with value 8 form the block's tail; equal values below 8 form one pair. The used rows of blocks 2k and 2k + 1 together number at most 384, reached by some two blocks, and some block has no unused row.
All inputs are finite; a program needn't handle non-finite values.
Results may differ from a plain program's by a relative error of at most 0.0055.
Values may be sent and summed in bfloat16 or wider, within the bound.
A program may use at most 64 MiB of HBM per device.

v0:
```python
import functools

import jax
import jax.numpy as jnp
from jax import lax
from jax.experimental import pallas as pl
from jax.experimental.pallas import tpu as pltpu
from jax.sharding import PartitionSpec as P

HEAD = 64
SLOTS = 8


def carried_in(part, axis, combine, identity):
    place = lax.axis_index(axis)
    gathered = lax.all_gather(part, axis)
    state = jnp.zeros_like(part) + jnp.asarray(identity, part.dtype)

    def one(step, state):
        return combine(state, lax.dynamic_index_in_dim(gathered, step, 0, False))

    return lax.fori_loop(0, place, one, state)


def attend_group(query_part, key_part, value_part, allowed):
    scores = jnp.einsum("qhd,khd->hqk", query_part, key_part, preferred_element_type=jnp.float32)
    masked = jnp.where(allowed[None], scores, -1e30)
    row_top = jnp.max(masked, axis=2, keepdims=True)
    exp_terms = jnp.where(allowed[None], jnp.exp(masked - row_top), 0.0)
    row_total = jnp.maximum(jnp.sum(exp_terms, axis=2, keepdims=True), 1.0)
    weights = (exp_terms / row_total).astype(jnp.bfloat16)
    mixed = jnp.einsum("hqk,khd->qhd", weights, value_part, preferred_element_type=jnp.float32)
    return mixed.astype(jnp.bfloat16)


def add_counts(earlier, later):
    return earlier + later


def shards(queries, key_rows, value_rows, pair_ids, out_weight, residual):
    cap_rows = queries.shape[0]
    local_width = queries.shape[1]
    heads_local = local_width // HEAD
    group_size = 4
    balanced_rows = residual.shape[0]
    allowed = (pair_ids[:, None] == pair_ids[None, :]) & (pair_ids[:, None] < SLOTS)

    def split_heads(stacked):
        return stacked.reshape(cap_rows, heads_local // group_size, group_size, HEAD).transpose(
            1, 0, 2, 3
        )

    def per_group(operands):
        return attend_group(operands[0], operands[1], operands[2], allowed)

    grouped = lax.map(
        per_group, (split_heads(queries), split_heads(key_rows), split_heads(value_rows))
    )
    attended = grouped.transpose(1, 0, 2, 3).reshape(cap_rows, local_width)
    live_rows = jnp.sum((pair_ids < SLOTS).astype(jnp.int32))
    devices = lax.axis_size("pairs")
    row_start = carried_in(live_rows.reshape(1), "pairs", add_counts, jnp.zeros((1,), jnp.int32))[0]
    partial_value = jnp.dot(
        attended,
        lax.all_gather(out_weight, "pairs", axis=1, tiled=True),
        preferred_element_type=jnp.float32,
    )
    payload = lax.psum_scatter(
        partial_value.astype(jnp.bfloat16), "tensor", scatter_dimension=1, tiled=True
    )
    per_peer = cap_rows // devices
    feature_width = payload.shape[1]
    peer_index = jnp.arange(devices, dtype=jnp.int32)
    turn_index = jnp.arange(per_peer, dtype=jnp.int32)
    source_rows = ((peer_index - row_start) % devices)[:, None] + devices * turn_index[None, :]
    slot_index = jnp.where(
        source_rows < live_rows, (row_start + source_rows) // devices, balanced_rows
    ).astype(jnp.int32)
    outgoing = jnp.take(payload, source_rows.reshape(-1), axis=0).reshape(
        devices, per_peer, feature_width
    )
    incoming = lax.all_to_all(outgoing, "pairs", split_axis=0, concat_axis=0, tiled=True)
    incoming_slots = lax.all_to_all(slot_index, "pairs", split_axis=0, concat_axis=0, tiled=True)
    landed = jnp.zeros((balanced_rows, feature_width), payload.dtype)
    moved_rows = landed.at[incoming_slots.reshape(-1)].set(
        incoming.reshape(-1, feature_width), mode="drop"
    )
    return (residual.astype(jnp.float32) + moved_rows.astype(jnp.float32)).astype(jnp.bfloat16)


HALVES = 2
PARTS = 4
WEIGHT_PIECES = 8
SPILL = 80
PAIR_CLASSES = 8
MESH = pl.DeviceIdType.MESH
BF16 = jnp.bfloat16
F32 = jnp.float32


def attend_pair(query_pair, key_pair, value_pair, bias):
    low = lax.broadcasted_iota(jnp.int32, query_pair.shape, 1) < HEAD
    zero = jnp.zeros_like(query_pair)
    one = jnp.ones_like(value_pair)
    queries = (jnp.where(low, query_pair, zero), jnp.where(low, zero, query_pair))
    values = (jnp.where(low, value_pair, one), jnp.where(low, one, value_pair))
    mixed = []
    for query_one, value_one in zip(queries, values):
        scores = lax.dot_general(
            query_one, key_pair, (((1,), (1,)), ((), ())), preferred_element_type=F32
        )
        masked = scores + bias
        exp_terms = jnp.exp(masked - jnp.max(masked, axis=1, keepdims=True)).astype(BF16)
        mixed.append(jnp.dot(exp_terms, value_one, preferred_element_type=F32))
    sums = jnp.where(low, mixed[0], mixed[1])
    totals = pltpu.roll(jnp.where(low, mixed[1], mixed[0]), HEAD, 1)
    return (sums / totals).astype(BF16)


def class_and_turn(place, per_class):
    kind = jnp.zeros_like(place)
    for bound in range(1, PAIR_CLASSES):
        kind = kind + jnp.where(place >= bound * per_class, 1, 0)
    return kind, place - per_class * kind


def fused_kernel(
    layers, tensors,
    q_hbm, k_hbm, v_hbm, ids_hbm, w_ref, res_hbm, out_ref,
    q_ref, k_ref, v_ref, ids_ref, res_ref,
    bias, acc, count_own, counts, w_full, attended, spilled, rows_all,
    core_out, core_in, mine, across_out, across_in, kept, summed, final_out, final_in,
    count_send, count_recv, w_send, w_recv, spill_send, spill_recv,
    own_send, relay_send, rows_recv, core_send, core_recv, across_send, across_recv,
    final_send, final_recv, load_sem, ids_sem, w_sem, res_sem,
):
    devices = layers * HALVES
    cap = q_ref.shape[0]
    width = q_ref.shape[1]
    half_rows = rows_all.shape[1]
    part_width = width // PARTS
    quarter = final_in.shape[2]
    per_class = half_rows // PAIR_CLASSES
    both = HALVES * half_rows
    p = lax.axis_index("pairs")
    t = lax.axis_index("tensor")
    z = p // HALVES
    y = p % HALVES
    x = t // 2
    core = t % 2
    beside = (z * HALVES + 1 - y, t)
    other_core = (p, x * 2 + 1 - core)
    other_chip = (p, (1 - x) * 2 + core)

    barrier = pltpu.get_barrier_semaphore()
    everyone = devices * tensors

    def greet(step, carry):
        number = lax.rem(p * tensors + t + step, everyone)
        pl.semaphore_signal(
            barrier, inc=1, device_id=(number // tensors, number % tensors), device_id_type=MESH
        )
        return carry

    loads = {}
    ids_load = pltpu.make_async_copy(ids_hbm, ids_ref, ids_sem)
    ids_load.start()
    for part in range(PARTS):
        columns = slice(part * part_width, (part + 1) * part_width)
        for which, (src, dst) in enumerate(((q_hbm, q_ref), (k_hbm, k_ref), (v_hbm, v_ref))):
            loads[part, which] = pltpu.make_async_copy(
                src.at[:, columns], dst.at[:, columns], load_sem.at[part, which]
            )
            loads[part, which].start()
    w_load = pltpu.make_async_copy(w_ref, w_full.at[y], w_sem)
    w_load.start()
    res_load = pltpu.make_async_copy(res_hbm, res_ref, res_sem)
    res_load.start()

    lax.fori_loop(1, everyone, greet, 0)
    ids_load.wait()

    ids_row = ids_ref[...].astype(F32)
    live = jnp.sum(jnp.where(ids_row < SLOTS, 1.0, 0.0), axis=1, keepdims=True)
    own_count = jnp.broadcast_to(live, count_own.shape).astype(jnp.int32)
    count_own[...] = own_count
    counts[p] = own_count
    ids_wide = jnp.broadcast_to(ids_row, (cap, cap))
    bias[...] = jnp.where(ids_wide == ids_wide.T, 0.0, -1e30)
    pl.semaphore_wait(barrier, everyone - 1)

    def remote(src, dst, sent, got, where_to):
        return pltpu.make_async_remote_copy(
            src_ref=src, dst_ref=dst, send_sem=sent, recv_sem=got,
            device_id=where_to, device_id_type=MESH,
        )

    pending = []
    for step in range(1, devices):
        peer = lax.rem(p + step, devices)
        copy = remote(count_own, counts.at[p], count_send.at[step], count_recv.at[p], (peer, t))
        copy.start()
        pending.append(copy)

    piece_rows = w_ref.shape[0] // WEIGHT_PIECES

    def weight_copy(piece, slot):
        rows = pl.ds(piece * piece_rows, piece_rows)
        return remote(
            w_ref.at[rows], w_full.at[slot, rows], w_send.at[piece], w_recv.at[piece], beside
        )

    def send_weights(first, last):
        for piece in range(first, last):
            copy = weight_copy(piece, y)
            copy.start()
            pending.append(copy)

    def rows_copy(block, part, sent, layer):
        here = rows_all.at[block, :, pl.ds(part * part_width, part_width)]
        return remote(here, here, sent, rows_recv.at[block, part], (layer * HALVES + y, t))

    spill_from = pl.multiple_of((1 - y) * (cap - SPILL), 16)

    def spill_copy(part):
        return remote(
            attended.at[pl.ds(spill_from, SPILL), pl.ds(part * part_width, part_width)], spilled.at[part],
            spill_send.at[part], spill_recv.at[part], beside,
        )

    def attend_part(part):
        for which in range(3):
            loads[part, which].wait()
        for pair in range(part_width // (2 * HEAD)):
            lanes = slice(part * part_width + pair * 2 * HEAD, part * part_width + (pair + 1) * 2 * HEAD)
            attended[:, lanes] = attend_pair(
                q_ref[:, lanes], k_ref[:, lanes], v_ref[:, lanes], bias[...]
            )
        copy = spill_copy(part)
        copy.start()
        pending.append(copy)

    send_weights(0, 2)
    attend_part(0)
    send_weights(2, 3)

    for step in range(1, devices):
        source = lax.rem(p + step, devices)
        remote(count_own, counts.at[source], count_send.at[0], count_recv.at[source], (source, t)).wait_recv()

    def start_of(block):
        total = jnp.zeros((1, cap), jnp.int32)
        for earlier in range(devices):
            total = total + jnp.where(earlier < block, counts[earlier, 0:1, :], 0)
        return total

    live_first = counts[HALVES * z, 0:1, :]
    live_second = counts[HALVES * z + 1, 0:1, :]
    second_at = both - live_second - ((both - live_first - live_second) & 7)
    start_pair = start_of(HALVES * z)
    kind, turn = class_and_turn(lax.broadcasted_iota(jnp.int32, (half_rows, cap), 0), per_class)
    slot = y * half_rows + ((kind - start_pair) & 7) + 8 * turn
    column = lax.broadcasted_iota(jnp.int32, (half_rows, cap), 1)
    row_first = slot
    row_second = slot - second_at
    row_own = jnp.where(y == 0, row_first, row_second)
    row_peer = jnp.where(y == 0, row_second, row_first)
    live_own = jnp.where(y == 0, live_first, live_second)
    live_peer = jnp.where(y == 0, live_second, live_first)
    pick_own = jnp.where((column == row_own) & (column < live_own), 1.0, 0.0).astype(BF16)
    peer_from = y * (cap - SPILL)
    pick_peer = jnp.where((column == row_peer - peer_from) & (column + peer_from < live_peer), 1.0, 0.0)
    pick_peer = pick_peer.astype(BF16)[:, :SPILL]

    def share_part(part):
        spill_copy(part).wait_recv()
        columns = slice(part * part_width, (part + 1) * part_width)
        packed = jnp.dot(pick_own, attended[:, columns], preferred_element_type=F32)
        packed = packed + jnp.dot(pick_peer, spilled[part], preferred_element_type=F32)
        rows_all[z, :, columns] = packed.astype(BF16)

        @pl.when(z < layers - 1)
        def _():
            rows_copy(z, part, own_send.at[0, part], z + 1).start()

        @pl.when(z > 0)
        def _():
            rows_copy(z, part, own_send.at[1, part], z - 1).start()

    share_part(0)
    for part in range(1, PARTS):
        attend_part(part)
        if part < PARTS - 1:
            send_weights(2 + part, 3 + part)
        share_part(part)
    send_weights(1 + PARTS, WEIGHT_PIECES)

    order = (
        z,
        jnp.where(z % 2 == 0, z + 1, z - 1),
        jnp.where(z < 2, 2, 1),
        jnp.where(z < 2, 3, 0),
    )
    inner = (z > 0) & (z < layers - 1)

    def take_rows(turn_index, relay):
        block = order[turn_index]
        onward = jnp.where(block < z, z + 1, z - 1)
        for part in range(PARTS):
            copy = rows_copy(block, part, relay_send.at[turn_index, part], onward)
            copy.wait_recv()
            if relay:
                copy.start()

    def take_inner(turn_index):
        @pl.when(inner)
        def _():
            take_rows(turn_index, True)

    def take_outer(turn_index):
        @pl.when(jnp.logical_not(inner))
        def _():
            take_rows(turn_index, False)

    def partial_of(turn_index, side, first=0, end=width):
        return jnp.dot(
            rows_all[order[turn_index], :, first:end], w_full[side, first:end, :],
            preferred_element_type=F32,
        )

    def core_copy(turn_index):
        return remote(
            core_out.at[turn_index], core_in.at[turn_index],
            core_send.at[turn_index], core_recv.at[turn_index], other_core,
        )

    def across_copy(turn_index):
        return remote(
            across_out.at[turn_index], across_in.at[turn_index],
            across_send.at[turn_index], across_recv.at[turn_index], other_chip,
        )

    def multiply(turn_index, side):
        hand_out(turn_index, side, partial_of(turn_index, side))

    def hand_out(turn_index, side, total):
        value = total.astype(BF16)

        @pl.when(core == side)
        def _():
            mine[turn_index] = value

        @pl.when(core != side)
        def _():
            core_out[turn_index] = value
            core_copy(turn_index).start()

    def add_cores(turn_index):
        core_copy(turn_index).wait_recv()
        total = mine[turn_index].astype(F32) + core_in[turn_index].astype(F32)
        left, right = total[:, :quarter], total[:, quarter:]
        across_out[turn_index] = jnp.where(x == 0, right, left).astype(BF16)
        kept[turn_index] = jnp.where(x == 0, left, right)
        across_copy(turn_index).start()

    def add_chips(turn_index):
        across_copy(turn_index).wait_recv()
        total = kept[turn_index] + across_in[turn_index].astype(F32)
        summed[:, order[turn_index]] = total.reshape(PAIR_CLASSES, per_class, quarter)

    last = layers - 1
    w_load.wait()
    multiply(0, y)
    for turn_index in range(1, last):
        take_inner(turn_index)
        take_outer(turn_index)
        multiply(turn_index, y)

        @pl.when(core == y)
        def _():
            add_cores(turn_index - 1)

    take_inner(last)

    @pl.when(core == y)
    def _():
        add_cores(last - 1)

    half_pieces = WEIGHT_PIECES // 2
    half_depth = width // 2
    for piece in range(half_pieces):
        weight_copy(piece, 1 - y).wait_recv()
    for turn_index in range(last):
        acc[turn_index] = partial_of(turn_index, 1 - y, 0, half_depth)
    for piece in range(half_pieces, WEIGHT_PIECES):
        weight_copy(piece, 1 - y).wait_recv()

    for turn_index in range(last):
        hand_out(
            turn_index, 1 - y,
            acc[turn_index] + partial_of(turn_index, 1 - y, half_depth, width),
        )

        @pl.when(core != y)
        def _():
            add_cores(turn_index)

    take_outer(last)
    core_out[last] = partial_of(last, 1 - core).astype(BF16)
    core_copy(last).start()
    mine[last] = partial_of(last, core).astype(BF16)
    add_cores(last)
    for turn_index in range(layers):
        add_chips(turn_index)

    final_out[...] = summed[...].reshape(final_out.shape).astype(BF16)
    source_slot = y * tensors + core * 2 + x
    to_self = z == t

    def final_copy(step):
        peer = lax.rem(p + step, devices)
        return remote(
            final_out.at[peer], final_in.at[source_slot],
            final_send.at[step], final_recv.at[source_slot], (peer, z),
        )

    for step in range(1, devices):
        copy = final_copy(step)
        copy.start()
        pending.append(copy)

    @pl.when(to_self)
    def _():
        final_in[source_slot] = final_out[p]

    @pl.when(jnp.logical_not(to_self))
    def _():
        final_copy(0).start()

    place_shape = (half_rows, HALVES * layers * per_class)
    lane = lax.broadcasted_iota(jnp.int32, (1, place_shape[1]), 1)
    side = jnp.where(lane >= layers * per_class, 1, 0)
    lane = lane - side * layers * per_class
    layer = jnp.zeros_like(lane)
    for bound in range(1, layers):
        layer = layer + jnp.where(lane >= bound * per_class, 1, 0)
    lane = lane - layer * per_class
    spot = jnp.zeros_like(lane) - 1
    count_width = place_shape[1]
    for block in range(layers):
        first = counts[HALVES * block, 0:1, :][:, :count_width]
        second = counts[HALVES * block + 1, 0:1, :][:, :count_width]
        begin = start_of(HALVES * block)[:, :count_width]
        second_from = both - second - ((both - first - second) & 7)
        where_at = side * half_rows + ((p - begin) & 7) + 8 * lane
        number = jnp.where(
            where_at < first, begin + where_at,
            jnp.where(
                (where_at >= second_from) & (where_at < second_from + second),
                begin + first + where_at - second_from, -8,
            ),
        )
        spot = jnp.where(layer == block, number >> 3, spot)
    place = jnp.where(
        lax.broadcasted_iota(jnp.int32, place_shape, 0) == spot, 1.0, 0.0
    ).astype(BF16)

    for half in range(HALVES):
        for piece in range(tensors):
            slot_index = half * tensors + piece
            from_self = (z == t) & (source_slot == slot_index)

            @pl.when(jnp.logical_not(from_self))
            def _():
                remote(
                    final_out.at[0], final_in.at[slot_index], final_send.at[0],
                    final_recv.at[slot_index], (lax.rem(p + 1, devices), t),
                ).wait_recv()

    res_load.wait()
    depth = layers * per_class
    for piece in range(tensors):
        columns = slice(piece * quarter, (piece + 1) * quarter)
        moved = res_ref[:, columns].astype(F32)
        for half in range(HALVES):
            moved = moved + jnp.dot(
                place[:, half * depth:(half + 1) * depth],
                final_in[half * tensors + piece], preferred_element_type=F32,
            )
        out_ref[:, columns] = moved.astype(BF16)

    for copy in pending:
        copy.wait_send()
    for turn_index in range(layers):
        core_copy(turn_index).wait_send()
        across_copy(turn_index).wait_send()
    for part in range(PARTS):
        @pl.when(z < layers - 1)
        def _():
            rows_copy(z, part, own_send.at[0, part], z + 1).wait_send()

        @pl.when(z > 0)
        def _():
            rows_copy(z, part, own_send.at[1, part], z - 1).wait_send()

    @pl.when(inner)
    def _():
        for turn_index in range(1, layers):
            block = order[turn_index]
            onward = jnp.where(block < z, z + 1, z - 1)
            for part in range(PARTS):
                rows_copy(block, part, relay_send.at[turn_index, part], onward).wait_send()

    @pl.when(jnp.logical_not(to_self))
    def _():
        final_copy(0).wait_send()


def fused_shards(layers, tensors, queries, key_rows, value_rows, pair_ids, out_weight, residual):
    devices = layers * HALVES
    cap, width = queries.shape
    half_rows = residual.shape[0]
    columns = out_weight.shape[1]
    quarter = columns // 2
    part_width = width // PARTS
    per_class = half_rows // PAIR_CLASSES
    depth = layers * per_class
    dma = pltpu.SemaphoreType.DMA
    vmem = pltpu.VMEM
    scratch = [
        vmem((cap, width), BF16), vmem((cap, width), BF16), vmem((cap, width), BF16),
        vmem((1, cap), jnp.int32),
        vmem(residual.shape, BF16),
        vmem((cap, cap), F32),
        vmem((layers - 1, half_rows, columns), F32),
        vmem((8, cap), jnp.int32),
        vmem((devices, 8, cap), jnp.int32),
        vmem((HALVES, width, columns), BF16),
        vmem((cap, width), BF16),
        vmem((PARTS, SPILL, part_width), BF16),
        vmem((layers, half_rows, width), BF16),
        vmem((layers, half_rows, columns), BF16),
        vmem((layers, half_rows, columns), BF16),
        vmem((layers, half_rows, columns), BF16),
        vmem((layers, half_rows, quarter), BF16),
        vmem((layers, half_rows, quarter), BF16),
        vmem((layers, half_rows, quarter), F32),
        vmem((PAIR_CLASSES, layers, per_class, quarter), F32),
        vmem((devices, depth, quarter), BF16),
        vmem((HALVES * tensors, depth, quarter), BF16),
        dma((devices,)), dma((devices,)),
        dma((WEIGHT_PIECES,)), dma((WEIGHT_PIECES,)),
        dma((PARTS,)), dma((PARTS,)),
        dma((2, PARTS)), dma((layers, PARTS)), dma((layers, PARTS)),
        dma((layers,)), dma((layers,)),
        dma((layers,)), dma((layers,)),
        dma((devices,)), dma((HALVES * tensors,)),
        dma((PARTS, 3)), dma, dma, dma,
    ]
    in_vmem = pl.BlockSpec(memory_space=pltpu.VMEM)
    return pl.pallas_call(
        functools.partial(fused_kernel, layers, tensors),
        out_shape=jax.ShapeDtypeStruct(residual.shape, residual.dtype),
        in_specs=[pl.BlockSpec(memory_space=pl.ANY)] * 6,
        out_specs=in_vmem,
        scratch_shapes=scratch,
        compiler_params=pltpu.CompilerParams(
            collective_id=0, has_side_effects=True, vmem_limit_bytes=56 * 1024 * 1024
        ),
    )(queries, key_rows, value_rows, pair_ids.reshape(1, cap), out_weight, residual)


def fits_fused(mesh):
    layers = mesh.shape["pairs"] // HALVES
    return mesh.shape["tensor"] == 4 and layers == 4


def solution(mesh):
    in_specs = (
        P("pairs", "tensor"),
        P("pairs", "tensor"),
        P("pairs", "tensor"),
        P("pairs"),
        P("tensor", "pairs"),
        P("pairs", "tensor"),
    )
    out_specs = P("pairs", "tensor")
    per_device = shards
    if fits_fused(mesh):
        per_device = functools.partial(fused_shards, mesh.shape["pairs"] // HALVES, mesh.shape["tensor"])
    return jax.shard_map(per_device, mesh=mesh, in_specs=in_specs, out_specs=out_specs, check_vma=False)
```

profile of v0, /device:TPU:24, one launch (start us, length us, event | category | flops | bytes accessed | tf_op | source)
XLA Modules:
  0.0 68.3 jit_solution(12884904876011525312)
XLA Ops:
  0.0 66.5 %shard_map.64 = bf16[192,1024]{1,0:T(8,128)(2,1)} custom-call(bf16[256,1024]{1,0:T(8,128)(2,1)} %q_hbm.1, bf16[256,1024]{1,0:T(8,128)(2,1)} %k_hbm.1, bf16[256,1024]{1,0:T(8,128)(2,1)} %v_hbm.1, s32[1,256]{1,0:T(1,128)} %bitcast.1, bf16[1024,512]{1,0:T(8,128)(2,1)} %w_ref.1, bf16[192,1024]{1,0:T(8,128)(2,1)} %res_hbm.1), custom_call_target="tpu_custom_call" | custom-call | tf_op jit(solution)/shard_map/pallas_call | solution.py:561
  66.5 1.8 %copy.8 = bf16[192,1024]{1,0:T(8,128)(2,1)} copy(bf16[192,1024]{1,0:T(8,128)(2,1)} %shard_map.64) | data formatting | bytes 786432
where the time goes:
time: 68.4 us; the launch traced here: 68.3 us
  Pallas kernels  66.5 us (97%)
  local copies, waits for them, and re-layouts  1.77 us (3%)
    pallas_call x1, Pallas kernels, fused_shards(): pl.pallas_call(functools.partial(fused_kernel, layers, tensors), out_shap...  66.5 us
    unnamed x1, local copies, waits for them, and re-layouts  1.77 us

commit v1 on v0

--- a/solution.py
+++ b/solution.py
@@ -137,7 +137,7 @@
     devices = layers * HALVES
     cap = q_ref.shape[0]
     width = q_ref.shape[1]
-    half_rows = rows_all.shape[1]
+    half_rows = rows_all.shape[2]
     part_width = width // PARTS
     quarter = final_in.shape[2]
     per_class = half_rows // PAIR_CLASSES
@@ -217,7 +217,7 @@
             pending.append(copy)
 
     def rows_copy(block, part, sent, layer):
-        here = rows_all.at[block, :, pl.ds(part * part_width, part_width)]
+        here = rows_all.at[block, part]
         return remote(here, here, sent, rows_recv.at[block, part], (layer * HALVES + y, t))
 
     spill_from = pl.multiple_of((1 - y) * (cap - SPILL), 16)
@@ -240,9 +240,10 @@
         copy.start()
         pending.append(copy)
 
-    send_weights(0, 2)
+    send_weights(0, 1)
     attend_part(0)
-    send_weights(2, 3)
+    attend_part(1)
+    send_weights(1, 2)
 
     for step in range(1, devices):
         source = lax.rem(p + step, devices)
@@ -277,7 +278,7 @@
         columns = slice(part * part_width, (part + 1) * part_width)
         packed = jnp.dot(pick_own, attended[:, columns], preferred_element_type=F32)
         packed = packed + jnp.dot(pick_peer, spilled[part], preferred_element_type=F32)
-        rows_all[z, :, columns] = packed.astype(BF16)
+        rows_all[z, part] = packed.astype(BF16)
 
         @pl.when(z < layers - 1)
         def _():
@@ -288,12 +289,14 @@
             rows_copy(z, part, own_send.at[1, part], z - 1).start()
 
     share_part(0)
-    for part in range(1, PARTS):
+    for part in range(2, PARTS):
         attend_part(part)
         if part < PARTS - 1:
-            send_weights(2 + part, 3 + part)
-        share_part(part)
-    send_weights(1 + PARTS, WEIGHT_PIECES)
+            send_weights(part, part + 1)
+        else:
+            send_weights(part, WEIGHT_PIECES)
+        share_part(part - 1)
+    share_part(PARTS - 1)
 
     order = (
         z,
@@ -323,10 +326,14 @@
             take_rows(turn_index, False)
 
     def partial_of(turn_index, side, first=0, end=width):
-        return jnp.dot(
-            rows_all[order[turn_index], :, first:end], w_full[side, first:end, :],
-            preferred_element_type=F32,
-        )
+        rows = jnp.concatenate(
+            [
+                rows_all[order[turn_index], part]
+                for part in range(first // part_width, end // part_width)
+            ],
+            axis=1,
+        )
+        return jnp.dot(rows, w_full[side, first:end, :], preferred_element_type=F32)
 
     def core_copy(turn_index):
         return remote(
@@ -538,7 +545,7 @@
         vmem((HALVES, width, columns), BF16),
         vmem((cap, width), BF16),
         vmem((PARTS, SPILL, part_width), BF16),
-        vmem((layers, half_rows, width), BF16),
+        vmem((layers, PARTS, half_rows, part_width), BF16),
         vmem((layers, half_rows, columns), BF16),
         vmem((layers, half_rows, columns), BF16),
         vmem((layers, half_rows, columns), BF16),

time: 68.4 us -> 61.5 us (0.90)
  Pallas kernels: 66.5 us -> 59.5 us
    pallas_call x1, Pallas kernels: 66.5 us -> 59.5 us  [fused_shards(): pl.pallas_call(functools.partial(fused_kernel, layers, tensors), out_shap...]
where the time goes in v1:
time: 61.5 us; the launch traced here: 61.3 us
  Pallas kernels  59.5 us (97%)
  local copies, waits for them, and re-layouts  1.77 us (3%)
    pallas_call x1, Pallas kernels, fused_shards(): pl.pallas_call(functools.partial(fused_kernel, layers, tensors), out_shap...  59.5 us
    unnamed x1, local copies, waits for them, and re-layouts  1.77 us

profile of v1, /device:TPU:24, one launch (start us, length us, event | category | flops | bytes accessed | tf_op | source)
XLA Modules:
  0.0 61.3 jit_solution(1255253716783672660)
XLA Ops:
  0.0 59.5 %shard_map.64 = bf16[192,1024]{1,0:T(8,128)(2,1)} custom-call(bf16[256,1024]{1,0:T(8,128)(2,1)} %q_hbm.1, bf16[256,1024]{1,0:T(8,128)(2,1)} %k_hbm.1, bf16[256,1024]{1,0:T(8,128)(2,1)} %v_hbm.1, s32[1,256]{1,0:T(1,128)} %bitcast.1, bf16[1024,512]{1,0:T(8,128)(2,1)} %w_ref.1, bf16[192,1024]{1,0:T(8,128)(2,1)} %res_hbm.1), custom_call_target="tpu_custom_call" | custom-call | tf_op jit(solution)/shard_map/pallas_call | solution.py:568
  59.5 1.8 %copy.8 = bf16[192,1024]{1,0:T(8,128)(2,1)} copy(bf16[192,1024]{1,0:T(8,128)(2,1)} %shard_map.64) | data formatting | bytes 786432

commit v2 on v1

--- a/solution.py
+++ b/solution.py
@@ -92,6 +92,7 @@
 PARTS = 4
 WEIGHT_PIECES = 8
 SPILL = 80
+BATCHES = 2
 PAIR_CLASSES = 8
 MESH = pl.DeviceIdType.MESH
 BF16 = jnp.bfloat16
@@ -139,7 +140,7 @@
     width = q_ref.shape[1]
     half_rows = rows_all.shape[2]
     part_width = width // PARTS
-    quarter = final_in.shape[2]
+    quarter = kept.shape[2]
     per_class = half_rows // PAIR_CLASSES
     both = HALVES * half_rows
     p = lax.axis_index("pairs")
@@ -298,12 +299,15 @@
         share_part(part - 1)
     share_part(PARTS - 1)
 
-    order = (
-        z,
-        jnp.where(z % 2 == 0, z + 1, z - 1),
-        jnp.where(z < 2, 2, 1),
-        jnp.where(z < 2, 3, 0),
-    )
+    def order_of(layer):
+        return (
+            layer,
+            jnp.where(layer % 2 == 0, layer + 1, layer - 1),
+            jnp.where(layer < 2, 2, 1),
+            jnp.where(layer < 2, 3, 0),
+        )
+
+    order = order_of(z)
     inner = (z > 0) & (z < layers - 1)
 
     def take_rows(turn_index, relay):
@@ -373,7 +377,35 @@
     def add_chips(turn_index):
         across_copy(turn_index).wait_recv()
         total = kept[turn_index] + across_in[turn_index].astype(F32)
-        summed[:, order[turn_index]] = total.reshape(PAIR_CLASSES, per_class, quarter)
+        summed[:, turn_index] = total.reshape(PAIR_CLASSES, per_class, quarter)
+
+    batch_turns = layers // BATCHES
+    batch_rows = batch_turns * per_class
+    source_slot = y * tensors + core * 2 + x
+    to_self = z == t
+
+    def final_copy(batch, step):
+        peer = lax.rem(p + step, devices)
+        return remote(
+            final_out.at[batch, peer], final_in.at[batch, source_slot],
+            final_send.at[batch, step], final_recv.at[batch, source_slot], (peer, z),
+        )
+
+    def spread(batch):
+        turns = slice(batch * batch_turns, (batch + 1) * batch_turns)
+        for turn_index in range(layers)[turns]:
+            add_chips(turn_index)
+        final_out[batch] = summed[:, turns].reshape(devices, batch_rows, quarter).astype(BF16)
+        for step in range(1, devices):
+            final_copy(batch, step).start()
+
+        @pl.when(to_self)
+        def _():
+            final_in[batch, source_slot] = final_out[batch, p]
+
+        @pl.when(jnp.logical_not(to_self))
+        def _():
+            final_copy(batch, 0).start()
 
     last = layers - 1
     w_load.wait()
@@ -392,6 +424,7 @@
     @pl.when(core == y)
     def _():
         add_cores(last - 1)
+        spread(0)
 
     half_pieces = WEIGHT_PIECES // 2
     half_depth = width // 2
@@ -412,37 +445,17 @@
         def _():
             add_cores(turn_index)
 
+    @pl.when(core != y)
+    def _():
+        spread(0)
+
     take_outer(last)
     core_out[last] = partial_of(last, 1 - core).astype(BF16)
     core_copy(last).start()
     mine[last] = partial_of(last, core).astype(BF16)
     add_cores(last)
-    for turn_index in range(layers):
-        add_chips(turn_index)
-
-    final_out[...] = summed[...].reshape(final_out.shape).astype(BF16)
-    source_slot = y * tensors + core * 2 + x
-    to_self = z == t
-
-    def final_copy(step):
-        peer = lax.rem(p + step, devices)
-        return remote(
-            final_out.at[peer], final_in.at[source_slot],
-            final_send.at[step], final_recv.at[source_slot], (peer, z),
-        )
-
-    for step in range(1, devices):
-        copy = final_copy(step)
-        copy.start()
-        pending.append(copy)
-
-    @pl.when(to_self)
-    def _():
-        final_in[source_slot] = final_out[p]
-
-    @pl.when(jnp.logical_not(to_self))
-    def _():
-        final_copy(0).start()
+    for batch in range(1, BATCHES):
+        spread(batch)
 
     place_shape = (half_rows, HALVES * layers * per_class)
     lane = lax.broadcasted_iota(jnp.int32, (1, place_shape[1]), 1)
@@ -454,7 +467,9 @@
     lane = lane - layer * per_class
     spot = jnp.zeros_like(lane) - 1
     count_width = place_shape[1]
-    for block in range(layers):
+    sender_order = order_of(t)
+    for turn_index in range(layers):
+        block = sender_order[turn_index]
         first = counts[HALVES * block, 0:1, :][:, :count_width]
         second = counts[HALVES * block + 1, 0:1, :][:, :count_width]
         begin = start_of(HALVES * block)[:, :count_width]
@@ -467,34 +482,32 @@
                 begin + first + where_at - second_from, -8,
             ),
         )
-        spot = jnp.where(layer == block, number >> 3, spot)
+        spot = jnp.where(layer == turn_index, number >> 3, spot)
     place = jnp.where(
         lax.broadcasted_iota(jnp.int32, place_shape, 0) == spot, 1.0, 0.0
     ).astype(BF16)
 
-    for half in range(HALVES):
-        for piece in range(tensors):
-            slot_index = half * tensors + piece
-            from_self = (z == t) & (source_slot == slot_index)
-
-            @pl.when(jnp.logical_not(from_self))
+    for batch in range(BATCHES):
+        for slot_index in range(HALVES * tensors):
+            @pl.when(jnp.logical_not(to_self & (source_slot == slot_index)))
             def _():
                 remote(
-                    final_out.at[0], final_in.at[slot_index], final_send.at[0],
-                    final_recv.at[slot_index], (lax.rem(p + 1, devices), t),
+                    final_out.at[batch, 0], final_in.at[batch, slot_index], final_send.at[batch, 0],
+                    final_recv.at[batch, slot_index], (lax.rem(p + 1, devices), t),
                 ).wait_recv()
 
     res_load.wait()
-    depth = layers * per_class
     for piece in range(tensors):
         columns = slice(piece * quarter, (piece + 1) * quarter)
-        moved = res_ref[:, columns].astype(F32)
-        for half in range(HALVES):
-            moved = moved + jnp.dot(
-                place[:, half * depth:(half + 1) * depth],
-                final_in[half * tensors + piece], preferred_element_type=F32,
-            )
-        out_ref[:, columns] = moved.astype(BF16)
+        rows = jnp.concatenate(
+            [
+                final_in[batch, half * tensors + piece]
+                for half in range(HALVES) for batch in range(BATCHES)
+            ],
+            axis=0,
+        )
+        moved = jnp.dot(place, rows, preferred_element_type=F32)
+        out_ref[:, columns] = (res_ref[:, columns].astype(F32) + moved).astype(BF16)
 
     for copy in pending:
         copy.wait_send()
@@ -518,9 +531,13 @@
             for part in range(PARTS):
                 rows_copy(block, part, relay_send.at[turn_index, part], onward).wait_send()
 
-    @pl.when(jnp.logical_not(to_self))
-    def _():
-        final_copy(0).wait_send()
+    for batch in range(BATCHES):
+        for step in range(1, devices):
+            final_copy(batch, step).wait_send()
+
+        @pl.when(jnp.logical_not(to_self))
+        def _():
+            final_copy(batch, 0).wait_send()
 
 
 def fused_shards(layers, tensors, queries, key_rows, value_rows, pair_ids, out_weight, residual):
@@ -531,7 +548,7 @@
     quarter = columns // 2
     part_width = width // PARTS
     per_class = half_rows // PAIR_CLASSES
-    depth = layers * per_class
+    batch_rows = layers // BATCHES * per_class
     dma = pltpu.SemaphoreType.DMA
     vmem = pltpu.VMEM
     scratch = [
@@ -553,15 +570,15 @@
         vmem((layers, half_rows, quarter), BF16),
         vmem((layers, half_rows, quarter), F32),
         vmem((PAIR_CLASSES, layers, per_class, quarter), F32),
-        vmem((devices, depth, quarter), BF16),
-        vmem((HALVES * tensors, depth, quarter), BF16),
+        vmem((BATCHES, devices, batch_rows, quarter), BF16),
+        vmem((BATCHES, HALVES * tensors, batch_rows, quarter), BF16),
         dma((devices,)), dma((devices,)),
         dma((WEIGHT_PIECES,)), dma((WEIGHT_PIECES,)),
         dma((PARTS,)), dma((PARTS,)),
         dma((2, PARTS)), dma((layers, PARTS)), dma((layers, PARTS)),
         dma((layers,)), dma((layers,)),
         dma((layers,)), dma((layers,)),
-        dma((devices,)), dma((HALVES * tensors,)),
+        dma((BATCHES, devices)), dma((BATCHES, HALVES * tensors)),
         dma((PARTS, 3)), dma, dma, dma,
     ]
     in_vmem = pl.BlockSpec(memory_space=pltpu.VMEM)

time: 61.5 us -> 61 us (level)
  no operation moved by 1% of the time
where the time goes in v2:
time: 61 us; the launch traced here: 60.8 us
  Pallas kernels  59.1 us (97%)
  local copies, waits for them, and re-layouts  1.77 us (3%)
    pallas_call x1, Pallas kernels, fused_shards(): pl.pallas_call(functools.partial(fused_kernel, layers, tensors), out_shap...  59.1 us
    unnamed x1, local copies, waits for them, and re-layouts  1.77 us

profile of v2, /device:TPU:24, one launch (start us, length us, event | category | flops | bytes accessed | tf_op | source)
XLA Modules:
  0.0 60.8 jit_solution(7327284200367288784)
XLA Ops:
  0.0 59.1 %shard_map.64 = bf16[192,1024]{1,0:T(8,128)(2,1)} custom-call(bf16[256,1024]{1,0:T(8,128)(2,1)} %q_hbm.1, bf16[256,1024]{1,0:T(8,128)(2,1)} %k_hbm.1, bf16[256,1024]{1,0:T(8,128)(2,1)} %v_hbm.1, s32[1,256]{1,0:T(1,128)} %bitcast.1, bf16[1024,512]{1,0:T(8,128)(2,1)} %w_ref.1, bf16[192,1024]{1,0:T(8,128)(2,1)} %res_hbm.1), custom_call_target="tpu_custom_call" | custom-call | tf_op jit(solution)/shard_map/pallas_call | solution.py:585
  59.1 1.8 %copy.8 = bf16[192,1024]{1,0:T(8,128)(2,1)} copy(bf16[192,1024]{1,0:T(8,128)(2,1)} %shard_map.64) | data formatting | bytes 786432

commit v3 on v2

--- a/solution.py
+++ b/solution.py
@@ -310,24 +310,19 @@
     order = order_of(z)
     inner = (z > 0) & (z < layers - 1)
 
-    def take_rows(turn_index, relay):
+    def take_row(turn_index, part, relay):
         block = order[turn_index]
         onward = jnp.where(block < z, z + 1, z - 1)
-        for part in range(PARTS):
-            copy = rows_copy(block, part, relay_send.at[turn_index, part], onward)
-            copy.wait_recv()
-            if relay:
-                copy.start()
-
-    def take_inner(turn_index):
-        @pl.when(inner)
-        def _():
-            take_rows(turn_index, True)
+        copy = rows_copy(block, part, relay_send.at[turn_index, part], onward)
+        copy.wait_recv()
+        if relay:
+            copy.start()
 
     def take_outer(turn_index):
         @pl.when(jnp.logical_not(inner))
         def _():
-            take_rows(turn_index, False)
+            for part in range(PARTS):
+                take_row(turn_index, part, False)
 
     def partial_of(turn_index, side, first=0, end=width):
         rows = jnp.concatenate(
@@ -408,18 +403,23 @@
             final_copy(batch, 0).start()
 
     last = layers - 1
+    @pl.when(inner)
+    def _():
+        for part in range(PARTS):
+            for turn_index in range(1, last):
+                take_row(turn_index, part, True)
+        for part in range(PARTS):
+            take_row(last, part, True)
+
     w_load.wait()
     multiply(0, y)
     for turn_index in range(1, last):
-        take_inner(turn_index)
         take_outer(turn_index)
         multiply(turn_index, y)
 
         @pl.when(core == y)
         def _():
             add_cores(turn_index - 1)
-
-    take_inner(last)
 
     @pl.when(core == y)
     def _():

time: 61 us -> 59.7 us (0.979)
  the two profiles are of different devices: /device:TPU:24 before, /device:TPU:25 now
where the time goes in v3:
time: 59.7 us; the launch traced here: 59.5 us
  Pallas kernels  57.8 us (97%)
  local copies, waits for them, and re-layouts  1.77 us (3%)
    pallas_call x1, Pallas kernels, fused_shards(): pl.pallas_call(functools.partial(fused_kernel, layers, tensors), out_shap...  57.8 us
    unnamed x1, local copies, waits for them, and re-layouts  1.77 us

profile of v3, /device:TPU:25, one launch (start us, length us, event | category | flops | bytes accessed | tf_op | source)
XLA Modules:
  0.0 59.5 jit_solution(11219051875380694258)
XLA Ops:
  0.0 57.8 %shard_map.64 = bf16[192,1024]{1,0:T(8,128)(2,1)} custom-call(bf16[256,1024]{1,0:T(8,128)(2,1)} %q_hbm.1, bf16[256,1024]{1,0:T(8,128)(2,1)} %k_hbm.1, bf16[256,1024]{1,0:T(8,128)(2,1)} %v_hbm.1, s32[1,256]{1,0:T(1,128)} %bitcast.1, bf16[1024,512]{1,0:T(8,128)(2,1)} %w_ref.1, bf16[192,1024]{1,0:T(8,128)(2,1)} %res_hbm.1), custom_call_target="tpu_custom_call" | custom-call | tf_op jit(solution)/shard_map/pallas_call | solution.py:585
  57.8 1.8 %copy.8 = bf16[192,1024]{1,0:T(8,128)(2,1)} copy(bf16[192,1024]{1,0:T(8,128)(2,1)} %shard_map.64) | data formatting | bytes 786432

commit v4 on v3

--- a/solution.py
+++ b/solution.py
@@ -241,10 +241,10 @@
         copy.start()
         pending.append(copy)
 
-    send_weights(0, 1)
+    send_weights(0, 2)
     attend_part(0)
     attend_part(1)
-    send_weights(1, 2)
+    send_weights(2, 3)
 
     for step in range(1, devices):
         source = lax.rem(p + step, devices)
@@ -293,9 +293,9 @@
     for part in range(2, PARTS):
         attend_part(part)
         if part < PARTS - 1:
-            send_weights(part, part + 1)
+            send_weights(part + 1, part + 2)
         else:
-            send_weights(part, WEIGHT_PIECES)
+            send_weights(part + 1, WEIGHT_PIECES)
         share_part(part - 1)
     share_part(PARTS - 1)
 

time: 59.7 us -> 62.5 us (1.047)
  Pallas kernels: 57.8 us -> 60.6 us
    pallas_call x1, Pallas kernels: 57.8 us -> 60.6 us  [fused_shards(): pl.pallas_call(functools.partial(fused_kernel, layers, tensors), out_shap...]
where the time goes in v4:
time: 62.5 us; the launch traced here: 62.4 us
  Pallas kernels  60.6 us (97%)
  local copies, waits for them, and re-layouts  1.77 us (3%)
    pallas_call x1, Pallas kernels, fused_shards(): pl.pallas_call(functools.partial(fused_kernel, layers, tensors), out_shap...  60.6 us
    unnamed x1, local copies, waits for them, and re-layouts  1.77 us

profile of v4, /device:TPU:25, one launch (start us, length us, event | category | flops | bytes accessed | tf_op | source)
XLA Modules:
  0.0 62.4 jit_solution(6789841348079562722)
XLA Ops:
  0.0 60.6 %shard_map.64 = bf16[192,1024]{1,0:T(8,128)(2,1)} custom-call(bf16[256,1024]{1,0:T(8,128)(2,1)} %q_hbm.1, bf16[256,1024]{1,0:T(8,128)(2,1)} %k_hbm.1, bf16[256,1024]{1,0:T(8,128)(2,1)} %v_hbm.1, s32[1,256]{1,0:T(1,128)} %bitcast.1, bf16[1024,512]{1,0:T(8,128)(2,1)} %w_ref.1, bf16[192,1024]{1,0:T(8,128)(2,1)} %res_hbm.1), custom_call_target="tpu_custom_call" | custom-call | tf_op jit(solution)/shard_map/pallas_call | solution.py:585
  60.6 1.8 %copy.8 = bf16[192,1024]{1,0:T(8,128)(2,1)} copy(bf16[192,1024]{1,0:T(8,128)(2,1)} %shard_map.64) | data formatting | bytes 786432
